TPU v7x, 128 devices: a whole 4x4x4 slice. The times are simulated.
128 devices in a mesh: inp: 16 (over y, z), tgt: 4 (over x_hi, core), mdl: 2 (over x_lo).
Axes of the slice: x: 4 (x_hi: 2, x_lo: 2; x = x_hi * 2 + x_lo), y: 4, z: 4, core: 2. Of those that a mesh axis runs over, the one named last changes fastest.
Arguments:
- encoder: bfloat16 [8192, 4096], P('inp'), may hold values from -8 to 8
- key_weight: bfloat16 [2, 4096, 2, 4, 256], P(None, None, 'mdl', 'tgt'), may hold values from -1 to 1
- value_weight: bfloat16 [2, 4096, 2, 4, 256], P(None, None, 'mdl', 'tgt'), may hold values from -0.09375 to 0.09375
- queries: bfloat16 [2, 2048, 8, 256], P(None, 'tgt', 'mdl'), may hold values from -8 to 8
- grad_out: bfloat16 [2, 2048, 8, 256], P(None, 'tgt', 'mdl'), may hold values from -6 to 6
Outputs:
- grad_query: bfloat16 [2, 2048, 8, 256], P(None, 'tgt', 'mdl')
- grad_encoder: bfloat16 [8192, 4096], P('inp', ('tgt', 'mdl'))
All inputs are finite; a program needn't handle non-finite values.
Results may differ from a plain program's by a relative error of at most 0.019.
The roundings to bfloat16 on the way count: a program that leaves them out, or rounds other values in their place, can miss the bound.
Values may be sent and summed in bfloat16 or wider, within the bound.
A program may use at most 128 MiB of HBM per device.

v0:
```python
import jax
import jax.numpy as jnp
from jax import lax
from jax.sharding import PartitionSpec as P


def joined(value, axis, join):
    pieces = jax.tree.map(lambda part: lax.all_gather(part, axis), value)
    head = jax.tree.map(lambda part: part[0], pieces)
    tail = jax.tree.map(lambda part: part[1:], pieces)
    total, _ = lax.scan(lambda total, slab: (join(total, slab), None), head, tail)
    return total


def combine_totals(one_side, other_side):
    peak_one, total_one, inner_one = one_side
    peak_two, total_two, inner_two = other_side
    peak_value = jnp.maximum(peak_one, peak_two)
    scale_one = jnp.exp(peak_one - peak_value)
    scale_two = jnp.exp(peak_two - peak_value)
    return (
        peak_value,
        total_one * scale_one + total_two * scale_two,
        inner_one * scale_one + inner_two * scale_two,
    )


def attention_grads(query_rows, grad_rows, key_block, value_block):
    scores = jnp.einsum("rhc,ehc->hre", query_rows, key_block, preferred_element_type=jnp.float32)
    local_peak = jnp.max(scores, axis=2)
    shifted = jnp.exp(scores - local_peak[:, :, None])
    dprobs = jnp.einsum("rhc,ehc->hre", grad_rows, value_block, preferred_element_type=jnp.float32)
    local_total = jnp.sum(shifted, axis=2)
    local_inner = jnp.sum(shifted * dprobs, axis=2)
    row_peak, row_total, row_inner = joined(
        (local_peak, local_total, local_inner), "inp", combine_totals
    )
    rescale = jnp.exp(local_peak - row_peak) / row_total
    attention = shifted * rescale[:, :, None]
    dscores = (attention * (dprobs - (row_inner / row_total)[:, :, None])).astype(jnp.bfloat16)
    attention_low = attention.astype(jnp.bfloat16)
    query_part = jnp.einsum("hre,ehc->rhc", dscores, key_block, preferred_element_type=jnp.float32)
    query_grad = lax.psum(query_part.astype(jnp.bfloat16), "inp")
    key_part = jnp.einsum("hre,rhc->ehc", dscores, query_rows, preferred_element_type=jnp.float32)
    value_part = jnp.einsum(
        "hre,rhc->ehc", attention_low, grad_rows, preferred_element_type=jnp.float32
    )
    return (query_grad, key_part, value_part)


def body(encoder, key_weight, value_weight, queries, grad_out):
    model_width = encoder.shape[1]
    enc_rows = encoder.shape[0]
    head_size = queries.shape[3]
    own_heads = key_weight.shape[2] * key_weight.shape[3]
    query_grads = []
    enc_terms = []
    for layer_index in range(queries.shape[0]):
        key_matrix = key_weight[layer_index].reshape(model_width, own_heads * head_size)
        value_matrix = value_weight[layer_index].reshape(model_width, own_heads * head_size)
        key_block = (
            jnp.dot(encoder, key_matrix, preferred_element_type=jnp.float32)
            .astype(jnp.bfloat16)
            .reshape(enc_rows, own_heads, head_size)
        )
        value_block = (
            jnp.dot(encoder, value_matrix, preferred_element_type=jnp.float32)
            .astype(jnp.bfloat16)
            .reshape(enc_rows, own_heads, head_size)
        )
        group_keys, group_values = (
            lax.all_gather(key_block, "tgt", axis=1, tiled=True),
            lax.all_gather(value_block, "tgt", axis=1, tiled=True),
        )
        query_grad, key_part, value_part = attention_grads(
            queries[layer_index], grad_out[layer_index], group_keys, group_values
        )
        key_total, value_total = (
            lax.psum_scatter(key_part, "tgt", scatter_dimension=1, tiled=True),
            lax.psum_scatter(value_part, "tgt", scatter_dimension=1, tiled=True),
        )
        query_grads.append(query_grad)
        key_flat = key_total.astype(jnp.bfloat16).reshape(enc_rows, own_heads * head_size)
        value_flat = value_total.astype(jnp.bfloat16).reshape(enc_rows, own_heads * head_size)
        enc_terms.append((key_flat, value_flat, key_matrix, value_matrix))
    share_rows = model_width // (lax.axis_size("tgt") * lax.axis_size("mdl"))
    running = jnp.zeros((share_rows * lax.axis_size(("tgt", "mdl")), enc_rows), jnp.float32)
    for key_flat, value_flat, key_matrix, value_matrix in enc_terms:
        running = running + jnp.einsum(
            "dc,ec->de", key_matrix, key_flat, preferred_element_type=jnp.float32
        )
        running = running + jnp.einsum(
            "dc,ec->de", value_matrix, value_flat, preferred_element_type=jnp.float32
        )
    enc_share = lax.psum_scatter(
        running.astype(jnp.bfloat16), ("tgt", "mdl"), scatter_dimension=0, tiled=True
    ).astype(jnp.float32)
    return (jnp.stack(query_grads), enc_share.T.astype(jnp.bfloat16))


def solution(mesh):
    placed = (
        P("inp", None),
        P(None, None, "mdl", "tgt", None),
        P(None, None, "mdl", "tgt", None),
        P(None, "tgt", "mdl", None),
        P(None, "tgt", "mdl", None),
    )
    return jax.shard_map(
        body,
        mesh=mesh,
        in_specs=placed,
        out_specs=(P(None, "tgt", "mdl", None), P("inp", ("tgt", "mdl"))),
        check_vma=False,
    )
```

profile of v0, /device:TPU:1, one launch (start us, length us, event | category | flops | bytes accessed | tf_op | source)
XLA Modules:
  0.0 549.1 jit_solution(9285284903059131960)
XLA Ops:
  7.2 0.0 all-gather.21.cloned.1.call-start
  7.2 4.8 fusion.50
  12.0 0.0 all-gather.21.cloned.1.call-update
  12.1 0.0 all-gather.23.cloned.1.call-start
  12.1 4.8 fusion.53
  17.0 0.0 all-gather.23.cloned.1.call-update
  17.0 0.0 all-gather.25.cloned.1.call-start
  17.0 4.8 fusion.56
  21.9 0.0 all-gather.25.cloned.1.call-update
  21.9 0.0 all-gather.27.cloned.1.call-start
  21.9 4.9 fusion.59
  26.8 0.0 all-gather.27.cloned.1.call-update
  26.9 0.0 reduce-scatter.10.cloned.1.call-start
  26.9 3.2 fusion.78
  30.1 2.6 fusion.79
  32.8 3.9 all-gather.21.cloned.1.call-done
  36.7 2.3 copy.39
  39.0 4.1 bitcast_reduce_fusion.1
  43.0 15.7 %all-gather.23.cloned.1.call-done = bf16[512,1024]{1,0:T(8,128)(2,1)} async-done(((bf16[512,256]{1,0:T(8,128)(2,1)}), bf16[512,1024]{1,0:T(8,128)(2,1)}) %all-gather.23.cloned.1.call-update) | async-done | bytes 1048592 | tf_op jit(solution)/shard_map/all_gather | solution.py:73
  58.7 5.6 %fusion.11 = (f32[4,512]{1,0:T(4,128)S(1)}, f32[4,512]{1,0:T(4,128)S(1)}, f32[4,512,512]{2,1,0:T(8,128)}) fusion(f32[4,512,512]{2,1,0:T(8,128)} %get-tuple-element.137, f32[4,512]{1,0:T(4,128)S(1)} %get-tuple-element.136, bf16[1,512,4,256]{3,2,1,0:T(4,128)(2,1)S(1)} %get-tuple-element.130, bf16[64,4,8,256]{3,2,1,0:T(8,128)(2,1)} %bitcast.230), kind=kOutput, calls=%fused_computation.28 | convolution fusion | flops 541061120 | bytes 10510336 | tf_op jit(solution)/shard_map/rhc,ehc->hre/dot_general | solution.py:32
  64.3 19.1 %all-gather.10 = f32[16,4,512]{2,1,0:T(4,128)S(1)} all-gather(f32[1,4,512]{2,1,0:T(4,128)S(1)} %bitcast.231), channel_id=3, replica_groups=mesh['inp'=16,'tgt'=4,'mdl'=2] {'inp'}, dimensions={0}, use_global_device_ids=true | all-gather | bytes 139264 | tf_op jit(solution)/shard_map/all_gather | solution.py:8
  83.4 19.0 %all-gather.11 = f32[16,4,512]{2,1,0:T(4,128)S(1)} all-gather(f32[1,4,512]{2,1,0:T(4,128)S(1)} %bitcast.235), channel_id=4, replica_groups=mesh['inp'=16,'tgt'=4,'mdl'=2] {'inp'}, dimensions={0}, use_global_device_ids=true | all-gather | bytes 139264 | tf_op jit(solution)/shard_map/all_gather | solution.py:8
  102.4 15.8 %all-gather.12 = f32[16,4,512]{2,1,0:T(4,128)S(1)} all-gather(f32[1,4,512]{2,1,0:T(4,128)S(1)} %bitcast.233), channel_id=6, replica_groups=mesh['inp'=16,'tgt'=4,'mdl'=2] {'inp'}, dimensions={0}, use_global_device_ids=true | all-gather | bytes 139264 | tf_op jit(solution)/shard_map/all_gather | solution.py:8
  118.2 0.0 all-gather.25.cloned.1.call-done
  118.2 1.5 copy.40
  119.8 2.9 bitcast_reduce_fusion
  122.7 18.4 %all-gather.13 = f32[16,4,512]{2,1,0:T(4,128)S(1)} all-gather(f32[1,4,512]{2,1,0:T(4,128)S(1)} %bitcast.232), channel_id=8, replica_groups=mesh['inp'=16,'tgt'=4,'mdl'=2] {'inp'}, dimensions={0}, use_global_device_ids=true | all-gather | bytes 139264 | tf_op jit(solution)/shard_map/all_gather | solution.py:8
  141.2 0.6 slice_bitcast_fusion.3
  141.8 5.5 fusion.7
  147.2 15.4 %all-gather.14 = f32[16,4,512]{2,1,0:T(4,128)S(1)} all-gather(f32[1,4,512]{2,1,0:T(4,128)S(1)} %bitcast.236), channel_id=9, replica_groups=mesh['inp'=16,'tgt'=4,'mdl'=2] {'inp'}, dimensions={0}, use_global_device_ids=true | all-gather | bytes 139264 | tf_op jit(solution)/shard_map/all_gather | solution.py:8
  162.7 18.1 %all-gather.15 = f32[16,4,512]{2,1,0:T(4,128)S(1)} all-gather(f32[1,4,512]{2,1,0:T(4,128)S(1)} %bitcast.234), channel_id=11, replica_groups=mesh['inp'=16,'tgt'=4,'mdl'=2] {'inp'}, dimensions={0}, use_global_device_ids=true | all-gather | bytes 139264 | tf_op jit(solution)/shard_map/all_gather | solution.py:8
  180.8 1.4 while.29
  182.2 0.6 copy-done.16
  182.8 4.7 fusion.9
  187.6 2.0 convolution_bitcast_fusion
  189.6 0.0 reduce-scatter.10.cloned.1.call-update
  189.6 0.0 reduce-scatter.8.cloned.1.call-start
  189.7 1.3 while.28
  191.1 4.7 fusion.47
  195.8 0.0 reduce-scatter.6.cloned.1.call-start
  195.8 4.7 fusion.13
  200.6 1.3 copy-done
  201.9 2.1 convolution_bitcast_fusion.1
  203.9 0.0 reduce-scatter.6.cloned.1.call-update
  204.0 0.0 reduce-scatter.12.cloned.1.call-start
  204.0 4.4 fusion.46
  208.5 0.0 all-reduce.3.cloned.1.call-start
  208.5 3.7 fusion.48
  212.2 1.7 fusion.49
  213.9 0.0 all-reduce.3.cloned.1.call-update
  213.9 0.3 reduce-scatter.14.cloned.1.call-start
  214.2 40.2 %reduce-scatter.10.cloned.1.call-done = f32[512,1,256]{2,0,1:T(8,128)} async-done(((f32[512,4,256]{2,0,1:T(8,128)}), f32[512,1,256]{2,0,1:T(8,128)}) %reduce-scatter.10.cloned.1.call-update) | async-done | bytes 524304 | tf_op jit(solution)/shard_map/reduce_scatter | solution.py:79
  254.4 6.3 %fusion.22 = f32[512,4096]{1,0:T(8,128)} fusion(bf16[2,4096,1,1,256]{4,1,3,2,0:T(8,128)(2,1)} %param.10, f32[512,1,256]{2,0,1:T(8,128)} %reduce-scatter.10.cloned.1.call-done), kind=kOutput, calls=%fused_computation.44 | convolution fusion | flops 1073872896 | bytes 11010048 | tf_op jit(solution)/shard_map/dc,ec->de/dot_general | solution.py:89
  260.7 34.2 %reduce-scatter.8.cloned.1.call-done = f32[512,1,256]{2,0,1:T(8,128)} async-done(((f32[512,4,256]{2,0,1:T(8,128)}), f32[512,1,256]{2,0,1:T(8,128)}) %reduce-scatter.8.cloned.1.call-update) | async-done | bytes 524304 | tf_op jit(solution)/shard_map/reduce_scatter | solution.py:80
  294.9 6.3 %fusion.26 = f32[512,4096]{1,0:T(8,128)} fusion(bf16[2,4096,1,1,256]{4,1,3,2,0:T(8,128)(2,1)} %param.11, f32[512,1,256]{2,0,1:T(8,128)} %reduce-scatter.8.cloned.1.call-done), kind=kOutput, calls=%fused_computation.48 | convolution fusion | flops 1073872896 | bytes 11010048 | tf_op jit(solution)/shard_map/dc,ec->de/dot_general | solution.py:92
  301.2 34.2 %reduce-scatter.6.cloned.1.call-done = f32[512,1,256]{2,0,1:T(8,128)} async-done(((f32[512,4,256]{2,0,1:T(8,128)}), f32[512,1,256]{2,0,1:T(8,128)}) %reduce-scatter.6.cloned.1.call-update) | async-done | bytes 524304 | tf_op jit(solution)/shard_map/reduce_scatter | solution.py:79
  335.4 6.3 %fusion.30 = f32[512,4096]{1,0:T(8,128)} fusion(bf16[2,4096,1,1,256]{4,1,3,2,0:T(8,128)(2,1)} %param.10, f32[512,1,256]{2,0,1:T(8,128)} %reduce-scatter.6.cloned.1.call-done), kind=kOutput, calls=%fused_computation.52 | convolution fusion | flops 1073872896 | bytes 11010048 | tf_op jit(solution)/shard_map/dc,ec->de/dot_general | solution.py:89
  341.7 34.3 %reduce-scatter.12.cloned.1.call-done = f32[512,1,256]{2,0,1:T(8,128)} async-done(((f32[512,4,256]{2,0,1:T(8,128)}), f32[512,1,256]{2,0,1:T(8,128)}) %reduce-scatter.12.cloned.1.call-update) | async-done | bytes 524304 | tf_op jit(solution)/shard_map/reduce_scatter | solution.py:80
  376.0 12.6 %fusion.6 = bf16[4096,512]{0,1:T(8,128)(2,1)} fusion(f32[512,4096]{1,0:T(8,128)} %fusion.22, f32[512,4096]{1,0:T(8,128)} %fusion.30, f32[512,4096]{1,0:T(8,128)} %fusion.26, bf16[2,4096,1,1,256]{4,1,3,2,0:T(8,128)(2,1)} %param.11, f32[512,1,256]{2,0,1:T(8,128)} %reduce-scatter.12.cloned.1.call-done), kind=kOutput, calls=%fused_computation.17 | convolution fusion | flops 1082261504 | bytes 31981568 | tf_op jit(solution)/shard_map/dc,ec->de/dot_general | solution.py:92
  388.6 0.0 reduce-scatter.14.cloned.1.call-update
  388.6 80.3 %all-reduce.3.cloned.1.call-done = (bf16[1,512,4,256]{1,3,2,0:T(8,128)(2,1)}, bf16[1,512,4,256]{1,3,2,0:T(8,128)(2,1)}) async-done(((bf16[1,512,4,256]{1,3,2,0:T(8,128)(2,1)}, bf16[1,512,4,256]{1,3,2,0:T(8,128)(2,1)}), (bf16[1,512,4,256]{1,3,2,0:T(8,128)(2,1)}, bf16[1,512,4,256]{1,3,2,0:T(8,128)(2,1)})) %all-reduce.3.cloned.1.call-update) | async-done | bytes 2097168 | tf_op jit(solution)/shard_map/psum | solution.py:43
  468.9 1.7 pad_maximum_fusion
  470.6 2.5 copy.32
  473.1 69.1 %reduce-scatter.14.cloned.1.call-done = bf16[512,512]{0,1:T(8,128)(2,1)} async-done(((bf16[4096,512]{0,1:T(8,128)(2,1)}), bf16[512,512]{0,1:T(8,128)(2,1)}) %reduce-scatter.14.cloned.1.call-update) | async-done | bytes 524304 | tf_op jit(solution)/shard_map/reduce_scatter | solution.py:95
  (143 shorter events, 2.0 us)
Async XLA Ops:
  7.2 29.6 %all-gather.21.cloned.1.call-start = ((), (), s32[]{:S(2)}) async-start(), calls=%async_computation.10 | async-start | bytes 1310720 | tf_op jit(solution)/shard_map/all_gather | solution.py:72
  12.1 46.6 %all-gather.23.cloned.1.call-start = ((), (), s32[]{:S(2)}) async-start(), calls=%async_computation.11 | async-start | bytes 1310720 | tf_op jit(solution)/shard_map/all_gather | solution.py:73
  17.0 101.3 %all-gather.25.cloned.1.call-start = ((), (), s32[]{:S(2)}) async-start(), calls=%async_computation.12 | async-start | bytes 1310720 | tf_op jit(solution)/shard_map/all_gather | solution.py:72
  21.9 119.9 %all-gather.27.cloned.1.call-start = ((), (), s32[]{:S(2)}) async-start(), calls=%async_computation.13 | async-start | bytes 1310720 | tf_op jit(solution)/shard_map/all_gather | solution.py:73
  26.9 227.6 %reduce-scatter.10.cloned.1.call-start = ((), (), s32[]{:S(2)}) async-start(), calls=%async_computation.7 | async-start | bytes 2621440 | tf_op jit(solution)/shard_map/reduce_scatter | solution.py:79
  30.1 12.9 %copy-start.2 = (bf16[1,512,4,256]{3,2,1,0:T(4,128)(2,1)}, bf16[1,512,4,256]{3,2,1,0:T(4,128)(2,1)S(1)}, u32[]{:S(2)}) copy-start(bf16[1,512,4,256]{3,2,1,0:T(4,128)(2,1)S(1)} %get-tuple-element.128) | copy-start | bytes 3145732
  32.8 25.9 %copy-start.1 = (bf16[1,512,4,256]{3,2,1,0:T(4,128)(2,1)}, bf16[1,512,4,256]{3,2,1,0:T(4,128)(2,1)S(1)}, u32[]{:S(2)}) copy-start(bf16[1,512,4,256]{3,2,1,0:T(4,128)(2,1)S(1)} %get-tuple-element.130) | copy-start | bytes 3145732
  43.0 21.3 %copy-start.12 = (f32[4,512]{1,0:T(4,128)}, f32[4,512]{1,0:T(4,128)S(1)}, u32[]{:S(2)}) copy-start(f32[4,512]{1,0:T(4,128)S(1)} %get-tuple-element.136) | copy-start | bytes 24580
  58.7 61.1 %copy-start.4 = (bf16[1,512,4,256]{3,2,1,0:T(4,128)(2,1)S(1)}, bf16[1,512,4,256]{3,2,1,0:T(4,128)(2,1)}, u32[]{:S(2)}) copy-start(bf16[1,512,4,256]{3,2,1,0:T(4,128)(2,1)} %get-tuple-element.129) | copy-start | bytes 3145732
  83.4 57.7 %copy-start.8 = (f32[16,4,512]{2,1,0:T(4,128)}, f32[16,4,512]{2,1,0:T(4,128)S(1)}, u32[]{:S(2)}) copy-start(f32[16,4,512]{2,1,0:T(4,128)S(1)} %all-gather.10) | copy-start | bytes 393220
  102.4 38.7 %copy-start.9 = (f32[16,4,512]{2,1,0:T(4,128)}, f32[16,4,512]{2,1,0:T(4,128)S(1)}, u32[]{:S(2)}) copy-start(f32[16,4,512]{2,1,0:T(4,128)S(1)} %all-gather.11) | copy-start | bytes 393220
  118.2 22.9 %copy-start.10 = (f32[16,4,512]{2,1,0:T(4,128)}, f32[16,4,512]{2,1,0:T(4,128)S(1)}, u32[]{:S(2)}) copy-start(f32[16,4,512]{2,1,0:T(4,128)S(1)} %all-gather.12) | copy-start | bytes 393220
  119.8 27.5 %copy-start.6 = (bf16[512,1024]{0,1:T(8,128)(2,1)}, bf16[512,1024]{0,1:T(8,128)(2,1)S(1)}, u32[]{:S(2)}) copy-start(bf16[512,1024]{0,1:T(8,128)(2,1)S(1)} %copy.40) | copy-start | bytes 3145732
  122.7 18.4 %copy-start.14 = (f32[4,512]{1,0:T(4,128)}, f32[4,512]{1,0:T(4,128)S(1)}, u32[]{:S(2)}) copy-start(f32[4,512]{1,0:T(4,128)S(1)} %get-tuple-element.139) | copy-start | bytes 24580
  141.8 40.4 %copy-start.15 = (f32[4,512]{1,0:T(4,128)S(1)}, f32[4,512]{1,0:T(4,128)}, u32[]{:S(2)}) copy-start(f32[4,512]{1,0:T(4,128)} %copy-done.14) | copy-start | bytes 24580
  182.2 0.6 copy-start.16
  182.8 4.7 copy-start.5
  187.5 2.1 slice-start
  187.5 2.1 slice-start.1
  187.5 2.1 slice-start.2
  187.6 2.1 copy-start.11
  187.6 3.5 copy-start.13
  189.6 105.3 %reduce-scatter.8.cloned.1.call-start = ((), (), s32[]{:S(2)}) async-start(), calls=%async_computation.6 | async-start | bytes 2621440 | tf_op jit(solution)/shard_map/reduce_scatter | solution.py:80
  195.8 139.6 %reduce-scatter.6.cloned.1.call-start = ((), (), s32[]{:S(2)}) async-start(), calls=%async_computation.5 | async-start | bytes 2621440 | tf_op jit(solution)/shard_map/reduce_scatter | solution.py:79
  195.8 6.0 %copy-start.3 = (bf16[1,512,4,256]{3,2,1,0:T(4,128)(2,1)S(1)}, bf16[1,512,4,256]{3,2,1,0:T(4,128)(2,1)}, u32[]{:S(2)}) copy-start(bf16[1,512,4,256]{3,2,1,0:T(4,128)(2,1)} %copy-done.2) | copy-start | bytes 3145732
  200.5 1.3 copy-start
  201.9 2.2 copy-start.17
  204.0 172.0 %reduce-scatter.12.cloned.1.call-start = ((), (), s32[]{:S(2)}) async-start(), calls=%async_computation.8 | async-start | bytes 2621440 | tf_op jit(solution)/shard_map/reduce_scatter | solution.py:80
  208.5 3.8 copy-start.7
  208.5 260.4 %all-reduce.3.cloned.1.call-start = ((), (), s32[]{:S(2)}) async-start(), calls=%async_computation.14 | async-start | bytes 4194304 | tf_op jit(solution)/shard_map/psum | solution.py:43
  213.9 328.3 %reduce-scatter.14.cloned.1.call-start = ((), (), s32[]{:S(2)}) async-start(), calls=%async_computation.9 | async-start | bytes 4718592 | tf_op jit(solution)/shard_map/reduce_scatter | solution.py:95
Sparse Core Ops, SparseCore 0:
  12.2 24.4 all-gather.20
  38.4 20.3 all-gather.22
  61.0 20.3 all-gather.24
  82.8 20.3 all-gather.26
  189.7 64.6 reduce-scatter.9
  257.1 37.7 reduce-scatter.7
  297.5 37.7 reduce-scatter.5
  338.2 37.7 reduce-scatter.11
  380.0 88.8 all-reduce.2
  471.8 70.3 reduce-scatter.13
where the time goes:
time: 550 us; the launch traced here: 549 us
  waiting for transfers between devices  312 us (57%)
  blocking collectives  106 us (19%)
  matrix products  87.5 us (16%)
  local copies, waits for them, and re-layouts  14.9 us (3%)
  between operations  14.5 us (3%)
  other arithmetic  12.9 us (2%)
    all_gather x6, blocking collectives, joined(): pieces = jax.tree.map(lambda part: lax.all_gather(part, axis), value)  106 us
    psum x1, waiting for transfers between devices, attention_grads(): query_grad = lax.psum(query_part.astype(jnp.bfloat16), 'inp')  80.3 us
    reduce_scatter x2, waiting for transfers between devices, body(): lax.psum_scatter(key_part, 'tgt', scatter_dimension=1, tiled=True)  74.4 us
    reduce_scatter x1, waiting for transfers between devices, body(): lax.psum_scatter(running.astype(jnp.bfloat16), ('tgt', 'mdl'), scatter_di...  69.1 us
    reduce_scatter x2, waiting for transfers between devices, body(): lax.psum_scatter(value_part, 'tgt', scatter_dimension=1, tiled=True)  68.4 us
    dot_general x2, matrix products, body(): jnp.einsum('dc,ec->de', value_matrix, value_flat, preferred_element_type=...  18.9 us
    all_gather x2, waiting for transfers between devices, body(): lax.all_gather(value_block, 'tgt', axis=1, tiled=True)  15.7 us
    dot_general x2, matrix products, body(): jnp.einsum('dc,ec->de', key_matrix, key_flat, preferred_element_type=jnp....  12.6 us
  transfers between devices with their start and end apart: 10, of which 8 were waited for; matrix products, arithmetic and copies ran while one was open for 17% of the time, Pallas kernels for 0%

commit v1 on v0

v1 whole, which is shorter than its diff:
```python
import functools

import jax
import jax.numpy as jnp
from jax import lax
from jax.experimental import pallas as pl
from jax.experimental.pallas import tpu as pltpu
from jax.sharding import PartitionSpec as P

MESH = pl.DeviceIdType.MESH
F32 = jnp.float32
BF16 = jnp.bfloat16
NT = (((1,), (1,)), ((), ()))

E = 512
D = 4096
C = 256
L = 2
N = 2048
CH = 8
NSEM = 128


def kernel(
    enc_hbm, kw_hbm, vw_hbm, q_hbm, g_hbm,
    dq_out, enc_out,
    enc, w, qg, kv, kt, pbuf, dpbuf, dsb, alb,
    stat_s, stat_r, stat_f,
    dqs, r1, s1, r2, dqt,
    grads, eb, cr, rl, nb,
    send_sems, recv_sems, local_sems,
):
    inp = lax.axis_index("inp")
    tgt = lax.axis_index("tgt")
    mdl = lax.axis_index("mdl")
    y, z = inp // 4, inp % 4
    xh, core = tgt // 2, tgt % 2
    x = xh * 2 + mdl

    def at_yz(yy, zz):
        return (yy * 4 + zz, tgt, mdl)

    def at_x(xx, cc):
        return (inp, (xx // 2) * 2 + cc, xx % 2)

    counter = [0]
    sent = []

    def put(src, dst, device):
        k = counter[0]
        counter[0] += 1
        cp = pltpu.make_async_remote_copy(
            src_ref=src, dst_ref=dst, send_sem=send_sems.at[k], recv_sem=recv_sems.at[k],
            device_id=device, device_id_type=MESH,
        )
        cp.start()
        sent.append(cp)
        return cp

    local_counter = [0]

    def load(src, dst):
        k = local_counter[0]
        local_counter[0] += 1
        cp = pltpu.make_async_copy(src, dst, local_sems.at[k])
        cp.start()
        return cp

    barrier = pltpu.get_barrier_semaphore()

    @pl.loop(1, 16)
    def _(o):
        pl.semaphore_signal(barrier, inc=1, device_id=((inp + o) % 16, tgt, mdl), device_id_type=MESH)

    @pl.loop(1, 8)
    def _(o):
        r = (tgt * 2 + mdl + o) % 8
        pl.semaphore_signal(barrier, inc=1, device_id=(inp, r // 2, r % 2), device_id_type=MESH)

    enc_load = load(enc_hbm, enc)
    own_q = load(q_hbm.at[tgt], qg.at[:, 0, :, :, tgt])
    own_g = load(g_hbm.at[tgt], qg.at[:, 1, :, :, tgt])
    w_loads = []
    for l in range(L):
        w_loads.append(load(kw_hbm.at[l], w.at[2 * l]))
        w_loads.append(load(vw_hbm.at[l], w.at[2 * l + 1]))

    stat_s[...] = jnp.zeros_like(stat_s)
    pl.semaphore_wait(barrier, 22)

    partner_t = xh * 2 + (1 - core)
    opp = (1 - xh) * 2
    x_phase, core_phase = [], []
    for r in range(2):
        there = opp + (core + r) % 2
        for k, src in enumerate((q_hbm, g_hbm)):
            x_phase.append(put(src.at[there, :, y, z], qg.at[:, k, y, z, tgt], (inp, there, mdl)))
    for k, src in enumerate((q_hbm, g_hbm)):
        core_phase.append(put(src.at[partner_t], qg.at[:, k, :, :, tgt], (inp, partner_t, mdl)))

    def plane_device(half, phase, d):
        if (half == 0) == (phase == 0):
            return at_yz((y + d) % 4, z)
        return at_yz(y, (z + d) % 4)

    def gather_phase(view, phase):
        out = []
        for d in range(1, 4):
            for half in range(2):
                if phase == 0:
                    ref = view(half, y, z)
                elif half == 0:
                    ref = view(half, slice(None), z)
                else:
                    ref = view(half, y, slice(None))
                out.append(put(ref, ref, plane_device(half, phase, d)))
        return out

    def arrive(cps):
        for cp in cps:
            cp.wait_recv()

    def qview(l):
        return lambda half, yy, zz: qg.at[l, half, yy, zz, pl.ds(opp, 2)]

    def project(j):
        w_loads[j].wait()
        val = jnp.dot(enc[...], w[j], preferred_element_type=F32).astype(BF16)
        kv[j] = val

    enc_load.wait()
    project(0)
    arrive(x_phase)
    q_a0 = gather_phase(qview(0), 0)
    project(1)
    q_a1 = gather_phase(qview(1), 0)
    arrive(q_a0)
    q_b0 = gather_phase(qview(0), 1)
    project(2)
    arrive(q_a1)
    q_b1 = gather_phase(qview(1), 1)
    project(3)
    for l in range(L):
        kt[l] = kv[2 * l].astype(F32).T.astype(BF16)
    own_q.wait()
    own_g.wait()
    arrive(core_phase)

    def scores(l, lo, hi):
        @pl.loop(lo, hi)
        def _(n):
            yy, zz = n // 2, (n % 2) * 2
            qc = qg[l, 0, yy, pl.ds(zz, 2)].reshape(256, C)
            gc = qg[l, 1, yy, pl.ds(zz, 2)].reshape(256, C)
            st = lax.dot_general(kv[2 * l], qc, NT, preferred_element_type=F32)
            dp = lax.dot_general(kv[2 * l + 1], gc, NT, preferred_element_type=F32)
            peak = jnp.max(st, axis=0, keepdims=True)
            p = jnp.exp(st - peak)
            pbuf[l, n] = p
            dpbuf[l, n] = dp
            total = jnp.sum(p, axis=0, keepdims=True)
            inner = jnp.sum(p * dp, axis=0, keepdims=True)
            for k in range(2):
                cols = slice(128 * k, 128 * k + 128)
                stat_s[l, 2 * n + k, 0:1, :] = peak[:, cols]
                stat_s[l, 2 * n + k, 1:2, :] = total[:, cols]
                stat_s[l, 2 * n + k, 2:3, :] = inner[:, cols]

    stat_sems = {}

    def stats_out(l, phase):
        k = counter[0]
        counter[0] += 1
        stat_sems[l, phase] = k

        @pl.loop(1, 16)
        def _(o):
            there = (inp + o) % 16
            if phase == 0:
                src, dst = stat_s.at[l, there], stat_r.at[l, o - 1]
            else:
                src, dst = stat_f.at[l, inp], stat_f.at[l, inp]
            pltpu.make_async_remote_copy(
                src_ref=src, dst_ref=dst, send_sem=send_sems.at[k], recv_sem=recv_sems.at[k],
                device_id=(there, tgt, mdl), device_id_type=MESH,
            ).start()

    def stats_in(l, phase, sems):
        k = stat_sems[l, phase]
        pltpu.make_async_copy(stat_r.at[l], stat_r.at[l], sems.at[k]).wait()

    def combine(l):
        stats_in(l, 0, recv_sems)
        own = stat_s[l, inp]
        got = stat_r[l]
        peaks = got[:, 0, :]
        peak = jnp.maximum(jnp.max(peaks, axis=0, keepdims=True), own[0:1])
        f = jnp.exp(peaks - peak)
        fo = jnp.exp(own[0:1] - peak)
        total = jnp.sum(got[:, 1, :] * f, axis=0, keepdims=True) + own[1:2] * fo
        inner = jnp.sum(got[:, 2, :] * f, axis=0, keepdims=True) + own[2:3] * fo
        stat_f[l, inp] = jnp.concatenate(
            [peak, total, inner / total, jnp.zeros((5, 128), F32)], axis=0
        )
        stats_out(l, 1)

    arrive(q_b0)
    scores(0, 0, CH)
    stats_out(0, 0)
    arrive(q_b1)
    scores(1, 0, CH // 2)
    combine(0)
    scores(1, CH // 2, CH)
    stats_out(1, 0)

    def dscores(l):
        stats_in(l, 1, recv_sems)

        @pl.loop(0, CH)
        def _(n):
            def row(ref, r):
                return jnp.concatenate([ref[l, 2 * n, r : r + 1], ref[l, 2 * n + 1, r : r + 1]], axis=1)

            fac = jnp.exp(row(stat_s, 0) - row(stat_f, 0)) / row(stat_f, 1)
            inner = row(stat_f, 2)
            a = pbuf[l, n] * fac
            ds = (a * (dpbuf[l, n] - inner)).astype(BF16)
            cols = pl.ds(pl.multiple_of(n * 256, 256), 256)
            dsb[:, cols] = ds
            alb[:, cols] = a.astype(BF16)
            dqc = jnp.dot(kt[l], ds, preferred_element_type=F32).astype(BF16)
            yy, zz = n // 2, (n % 2) * 2
            for half in range(2):
                for k in range(2):
                    dqs[l, half, yy, zz + k] = dqc[128 * half : 128 * half + 128, 128 * k : 128 * k + 128]

    def kv_grads(l):
        qf = qg[l, 0].reshape(N, C)
        gf = qg[l, 1].reshape(N, C)
        grads[2 * l] = jnp.dot(dsb[...], qf, preferred_element_type=F32).astype(BF16)
        grads[2 * l + 1] = jnp.dot(alb[...], gf, preferred_element_type=F32).astype(BF16)

    def rs_first(l):
        out = []
        for d in range(1, 4):
            out.append(put(dqs.at[l, 0, (y + d) % 4], r1.at[l, 0, d - 1], plane_device(0, 0, d)))
            out.append(put(dqs.at[l, 1, :, (z + d) % 4], r1.at[l, 1, d - 1], plane_device(1, 0, d)))
        return out

    def rs_second(l, first):
        arrive(first)
        for half in range(2):
            own = dqs[l, 0, y] if half == 0 else dqs[l, 1, :, z]
            acc = own.astype(F32)
            for d in range(3):
                acc = acc + r1[l, half, d].astype(F32)
            s1[l, half] = acc.astype(BF16)
        out = []
        for d in range(1, 4):
            out.append(put(s1.at[l, 0, (z + d) % 4], r2.at[l, 0, d - 1], plane_device(0, 1, d)))
            out.append(put(s1.at[l, 1, (y + d) % 4], r2.at[l, 1, d - 1], plane_device(1, 1, d)))
        return out

    def rs_end(l, second):
        arrive(second)
        for half in range(2):
            acc = (s1[l, 0, z] if half == 0 else s1[l, 1, y]).astype(F32)
            for d in range(3):
                acc = acc + r2[l, half, d].astype(F32)
            dqt[l, :, :, 128 * half : 128 * half + 128] = acc.T.reshape(4, 32, 128).astype(BF16)
        out = [
            put(dqt.at[l, (tgt + d) % 4], dq_out.at[l, tgt, y, z], (inp, (tgt + d) % 4, mdl))
            for d in range(1, 4)
        ]
        mine = load(dqt.at[l, tgt], dq_out.at[l, tgt, y, z])
        return out, mine

    def oview(l):
        return lambda half, yy, zz: dq_out.at[l, pl.ds(2 * half, 2), yy, zz]

    dscores(0)
    f0 = rs_first(0)
    combine(1)
    kv_grads(0)
    e0 = rs_second(0, f0)
    dscores(1)
    f1 = rs_first(1)
    x0, m0 = rs_end(0, e0)
    kv_grads(1)

    def block(xx, cc):
        f = (xx // 2) * 4 + cc * 2 + xx % 2
        rows = pl.ds(pl.multiple_of(f * 512, 512), 512)
        acc = lax.dot_general(grads[0], w[0, rows, :], NT, preferred_element_type=F32)
        for j in range(1, 4):
            acc = acc + lax.dot_general(grads[j], w[j, rows, :], NT, preferred_element_type=F32)
        return acc.astype(BF16)

    def both(k, xx):
        eb[k, 0] = block(xx, 1 - core)
        cp = put(eb.at[k, 0], cr.at[k], at_x(x, 1 - core))
        eb[k, 1] = block(xx, core)
        return cp

    xp, xm, xo = (x + 1) % 4, (x + 3) % 4, (x + 2) % 4

    arrive(x0)
    m0.wait()
    a0 = gather_phase(oview(0), 0)
    c_o = both(0, xo)
    e1 = rs_second(1, f1)
    arrive([c_o])
    eb[0, 1] = eb[0, 1] + cr[0]
    ro = [
        put(eb.at[0, 1, pl.ds(0, 256)], rl.at[0], at_x(xp, core)),
        put(eb.at[0, 1, pl.ds(256, 256)], rl.at[1], at_x(xm, core)),
    ]
    arrive(a0)
    b0 = gather_phase(oview(0), 1)
    c_p = both(1, xp)
    c_m = both(2, xm)
    arrive([c_p, c_m])
    eb[1, 1] = eb[1, 1] + cr[1]
    eb[2, 1] = eb[2, 1] + cr[2]
    n1 = [
        put(eb.at[1, 1, pl.ds(256, 256)], nb.at[0, pl.ds(256, 256)], at_x(xp, core)),
        put(eb.at[2, 1, pl.ds(0, 256)], nb.at[1, pl.ds(0, 256)], at_x(xm, core)),
    ]
    x1, m1 = rs_end(1, e1)
    arrive(ro)
    eb[1, 1, 0:256] = eb[1, 1, 0:256] + rl[0]
    eb[2, 1, 256:512] = eb[2, 1, 256:512] + rl[1]
    n2 = [
        put(eb.at[1, 1, pl.ds(0, 256)], nb.at[0, pl.ds(0, 256)], at_x(xp, core)),
        put(eb.at[2, 1, pl.ds(256, 256)], nb.at[1, pl.ds(256, 256)], at_x(xm, core)),
    ]
    c_s = both(3, x)
    arrive(x1)
    m1.wait()
    a1 = gather_phase(oview(1), 0)
    arrive([c_s])
    arrive(a1)
    b1 = gather_phase(oview(1), 1)
    arrive(n1)
    arrive(n2)
    enc_out[...] = (
        eb[3, 1].astype(F32) + cr[3].astype(F32) + nb[0].astype(F32) + nb[1].astype(F32)
    ).astype(BF16)
    arrive(b0)
    arrive(b1)
    for cp in sent:
        cp.wait_send()
    for (l, phase) in stat_sems:
        stats_in(l, phase, send_sems)


def body(encoder, key_weight, value_weight, queries, grad_out):
    kw = key_weight.reshape(L, D, C)
    vw = value_weight.reshape(L, D, C)
    q = jnp.transpose(queries, (2, 0, 1, 3)).reshape(4, L, 4, 4, 32, C)
    g = jnp.transpose(grad_out, (2, 0, 1, 3)).reshape(4, L, 4, 4, 32, C)
    anywhere = pl.BlockSpec(memory_space=pl.ANY)
    dq, de = pl.pallas_call(
        kernel,
        out_shape=(
            jax.ShapeDtypeStruct((L, 4, 4, 4, 32, C), BF16),
            jax.ShapeDtypeStruct((E, 512), BF16),
        ),
        in_specs=[anywhere] * 5,
        out_specs=(anywhere, pl.BlockSpec(memory_space=pltpu.VMEM)),
        scratch_shapes=[
            pltpu.VMEM((E, D), BF16),
            pltpu.VMEM((4, D, C), BF16),
            pltpu.VMEM((L, 2, 4, 4, 4, 32, C), BF16),
            pltpu.VMEM((4, E, C), BF16),
            pltpu.VMEM((L, C, E), BF16),
            pltpu.VMEM((L, CH, E, 256), F32),
            pltpu.VMEM((L, CH, E, 256), F32),
            pltpu.VMEM((E, N), BF16),
            pltpu.VMEM((E, N), BF16),
            pltpu.VMEM((L, 16, 8, 128), F32),
            pltpu.VMEM((L, 15, 8, 128), F32),
            pltpu.VMEM((L, 16, 8, 128), F32),
            pltpu.VMEM((L, 2, 4, 4, 128, 128), BF16),
            pltpu.VMEM((L, 2, 3, 4, 128, 128), BF16),
            pltpu.VMEM((L, 2, 4, 128, 128), BF16),
            pltpu.VMEM((L, 2, 3, 128, 128), BF16),
            pltpu.VMEM((L, 4, 32, C), BF16),
            pltpu.VMEM((4, E, C), BF16),
            pltpu.VMEM((4, 2, E, 512), BF16),
            pltpu.VMEM((4, E, 512), BF16),
            pltpu.VMEM((2, 256, 512), BF16),
            pltpu.VMEM((2, E, 512), BF16),
            pltpu.SemaphoreType.DMA((NSEM,)),
            pltpu.SemaphoreType.DMA((NSEM,)),
            pltpu.SemaphoreType.DMA((16,)),
        ],
        compiler_params=pltpu.CompilerParams(
            collective_id=0, has_side_effects=True, vmem_limit_bytes=60 * 2**20
        ),
        cost_estimate=pl.CostEstimate(flops=14_000_000_000, bytes_accessed=20_000_000, transcendentals=2_000_000),
    )(encoder, kw, vw, q, g)
    dq = jnp.transpose(dq.reshape(L, 4, 512, C), (0, 2, 1, 3))
    return dq, de


def solution(mesh):
    placed = (
        P("inp", None),
        P(None, None, "mdl", "tgt", None),
        P(None, None, "mdl", "tgt", None),
        P(None, "tgt", "mdl", None),
        P(None, "tgt", "mdl", None),
    )
    return jax.shard_map(
        body,
        mesh=mesh,
        in_specs=placed,
        out_specs=(P(None, "tgt", "mdl", None), P("inp", ("tgt", "mdl"))),
        check_vma=False,
    )
```

time: 550 us -> 102 us (0.19)
  waiting for transfers between devices: 312 us -> 0 us
  blocking collectives: 106 us -> 0 us
  Pallas kernels: 0 us -> 91.1 us
  matrix products: 87.5 us -> 0 us
  between operations: 14.5 us -> 0.66 us
  other arithmetic: 12.9 us -> 0 us
    reduce_scatter x5 -> x0, waiting for transfers between devices: 212 us -> none  [the longest x2 74.4 us: body(): lax.psum_scatter(key_part, 'tgt', scatter_dimension=1, tiled=True)]
    all_gather x6 -> x0, blocking collectives: 106 us -> none  [joined(): pieces = jax.tree.map(lambda part: lax.all_gather(part, axis), value)]
    pallas_call x0 -> x1, Pallas kernels: none -> 91.1 us  [body(): pl.pallas_call(kernel, out_shape=(jax.ShapeDtypeStruct((L, 4, 4, 4, 32, C...]
    dot_general x18 -> x0, matrix products: 87.5 us -> none  [the longest x2 18.9 us: body(): jnp.einsum('dc,ec->de', value_matrix, value_flat, preferred_element_type=...]
    psum x1 -> x0, waiting for transfers between devices: 80.3 us -> none  [attention_grads(): query_grad = lax.psum(query_part.astype(jnp.bfloat16), 'inp')]
    all_gather x4 -> x0, waiting for transfers between devices: 19.6 us -> none  [the longest x2 15.7 us: body(): lax.all_gather(value_block, 'tgt', axis=1, tiled=True)]
    convert_element_type x2 -> x0, other arithmetic: 9.4 us -> none  [attention_grads(): (attention * (dprobs - (row_inner / row_total)[:, :, None])).astype(jnp.b...]
    slice x17 -> x0, local copies, waits for them, and re-layouts: 6.52 us -> none  [the longest x1 3.23 us: body(): queries[layer_index]]
  transfers between devices with their start and end apart: 10 -> 0, of which waited for: 8 -> 0; matrix products, arithmetic and copies ran while one was open for 17% -> 0% of each run, Pallas kernels for 0% -> 0%
where the time goes in v1:
time: 102 us
  Pallas kernels  91.1 us (89%)
  local copies, waits for them, and re-layouts  10.3 us (10%)
    pallas_call x1, Pallas kernels, body(): pl.pallas_call(kernel, out_shape=(jax.ShapeDtypeStruct((L, 4, 4, 4, 32, C...  91.1 us
    reshape x1, local copies, waits for them, and re-layouts, body(): dq = jnp.transpose(dq.reshape(L, 4, 512, C), (0, 2, 1, 3))  4.59 us
    transpose x1, local copies, waits for them, and re-layouts, body(): q = jnp.transpose(queries, (2, 0, 1, 3)).reshape(4, L, 4, 4, 32, C)  3.33 us

profile of v1, /device:TPU:1, one launch (start us, length us, event | category | flops | bytes accessed | tf_op | source)
XLA Modules:
  0.0 102.1 jit_solution(16238866836938404776)
XLA Ops:
  0.6 0.0 copy-start
  0.6 3.3 %copy.7 = bf16[4,2,512,256]{3,2,1,0:T(8,128)(2,1)} copy(bf16[4,2,512,256]{3,0,2,1:T(4,128)(2,1)} %bitcast.10) | data formatting | bytes 4194304 | tf_op jit(solution)/shard_map/transpose | solution.py:360
  4.0 0.0 copy-done
  4.0 1.6 %copy.8 = bf16[4,2,512,256]{3,2,1,0:T(8,128)(2,1)} copy(bf16[4,2,512,256]{3,0,2,1:T(4,128)(2,1)S(1)} %bitcast.11) | data formatting | bytes 4194304 | tf_op jit(solution)/shard_map/transpose | solution.py:361
  5.6 91.1 %shard_map.68 = (bf16[2,4,4,4,32,256]{5,4,3,2,1,0:T(8,128)(2,1)}, bf16[512,512]{1,0:T(8,128)(2,1)}) custom-call(bf16[512,4096]{1,0:T(8,128)(2,1)} %enc_hbm.1, bf16[2,4096,256]{2,1,0:T(8,128)(2,1)} %bitcast.16, bf16[2,4096,256]{2,1,0:T(8,128)(2,1)} %bitcast.17, bf16[4,2,4,4,32,256]{5,4,3,2,1,0:T(8,128)(2,1)} %bitcast.14, bf16[4,2,4,4,32,256]{5,4,3,2,1,0:T(8,128)(2,1)} %bitcast.15), custom_call_target="tpu_custom_call" | custom-call | flops 14000000000 | bytes 20000000 | tf_op jit(solution)/shard_map/pallas_call | solution.py:363
  96.7 0.0 copy-start.1
  96.8 4.6 %copy.11 = bf16[2,4,512,256]{3,1,2,0:T(4,128)(2,1)} copy(bf16[2,4,512,256]{3,2,1,0:T(8,128)(2,1)} %bitcast.13) | data formatting | bytes 4194304 | tf_op jit(solution)/shard_map/reshape | solution.py:403
  101.3 0.0 copy-done.1
  101.3 0.8 copy.13
Async XLA Ops:
  0.6 3.3 %copy-start = (bf16[2,512,4,256]{3,2,1,0:T(4,128)(2,1)S(1)}, bf16[2,512,4,256]{3,2,1,0:T(4,128)(2,1)}, u32[]{:S(2)}) copy-start(bf16[2,512,4,256]{3,2,1,0:T(4,128)(2,1)} %param.9) | copy-start | bytes 6291460
  96.7 4.6 %copy-start.1 = (bf16[512,512]{1,0:T(8,128)(2,1)S(1)}, bf16[512,512]{1,0:T(8,128)(2,1)}, u32[]{:S(2)}) copy-start(bf16[512,512]{1,0:T(8,128)(2,1)} %get-tuple-element.9) | copy-start | bytes 1572868

commit v2 on v1

v2 whole, which is shorter than its diff:
```python
import functools

import jax
import jax.numpy as jnp
from jax import lax
from jax.experimental import pallas as pl
from jax.experimental.pallas import tpu as pltpu
from jax.sharding import PartitionSpec as P

MESH = pl.DeviceIdType.MESH
F32 = jnp.float32
BF16 = jnp.bfloat16
NT = (((1,), (1,)), ((), ()))

E = 512
D = 4096
C = 256
L = 2
N = 2048
NSEM = 128


def kernel(
    enc_hbm, kw_hbm, vw_hbm, q_hbm, g_hbm,
    dq_out, enc_out,
    enc, w, qg, kv, kt, pbuf, dpbuf, dsb, alb,
    stat_s, stat_r, stat_c, fac, inn,
    dqs, r1, s1, r2, dqt, ob,
    kvacc, grads, eb, cr, rl, nb,
    send_sems, recv_sems, local_sems,
):
    inp = lax.axis_index("inp")
    tgt = lax.axis_index("tgt")
    mdl = lax.axis_index("mdl")
    y, z = inp // 4, inp % 4
    xh, core = tgt // 2, tgt % 2
    x = xh * 2 + mdl
    opp = (1 - xh) * 2
    partner = xh * 2 + (1 - core)
    xp, xm, xo = (x + 1) % 4, (x + 3) % 4, (x + 2) % 4

    def at_yz(yy, zz):
        return (yy * 4 + zz, tgt, mdl)

    def at_x(xx, cc):
        return (inp, (xx // 2) * 2 + cc, xx % 2)

    counter = [0]
    sent = []

    def put(src, dst, device):
        k = counter[0]
        counter[0] += 1
        cp = pltpu.make_async_remote_copy(
            src_ref=src, dst_ref=dst, send_sem=send_sems.at[k], recv_sem=recv_sems.at[k],
            device_id=device, device_id_type=MESH,
        )
        cp.start()
        sent.append(cp)
        return cp

    local_counter = [0]

    def load(src, dst):
        k = local_counter[0]
        local_counter[0] += 1
        cp = pltpu.make_async_copy(src, dst, local_sems.at[k])
        cp.start()
        return cp

    def arrive(cps):
        for cp in cps:
            cp.wait_recv()

    barrier = pltpu.get_barrier_semaphore()
    friends = [at_yz((y + d) % 4, z) for d in range(1, 4)] + [at_yz(y, (z + d) % 4) for d in range(1, 4)]
    friends += [(inp, partner, mdl), (inp, opp, mdl), (inp, opp + 1, mdl), at_x(xp, core), at_x(xm, core)]
    for friend in friends:
        pl.semaphore_signal(barrier, inc=1, device_id=friend, device_id_type=MESH)

    enc_load = load(enc_hbm, enc)
    w_loads = []
    for l in range(L):
        w_loads.append(
            (load(kw_hbm.at[l], w.at[l, :, pl.ds(0, C)]), load(vw_hbm.at[l], w.at[l, :, pl.ds(C, C)]))
        )
        if l == 0:
            own = [load(src.at[tgt], qg.at[:, k, 0, :, :, core]) for k, src in enumerate((q_hbm, g_hbm))]

    def plane_device(half, phase, d):
        if (half == 0) == (phase == 0):
            return at_yz((y + d) % 4, z)
        return at_yz(y, (z + d) % 4)

    def gather_phase(view, phase):
        out = []
        for d in range(1, 4):
            for half in range(2):
                if phase == 0:
                    ref = view(half, y, z)
                elif half == 0:
                    ref = view(half, slice(None), z)
                else:
                    ref = view(half, y, slice(None))
                out.append(put(ref, ref, plane_device(half, phase, d)))
        return out

    def qview(l):
        if l == 0:
            return lambda half, yy, zz: qg.at[0, half, 1, yy, zz]
        return lambda half, yy, zz: qg.at[1, 0, 1, yy, zz, half]

    def project(l):
        for cp in w_loads[l]:
            cp.wait()
        kv[l] = jnp.dot(enc[...], w[l], preferred_element_type=F32).astype(BF16)
        kt[l] = kv[l, :, 0:C].astype(F32).T.astype(BF16)

    def scores(grp, l):
        @pl.loop(0, 4)
        def _(n):
            qc = qg[l, 0, grp, n].reshape(256, C)
            gc = qg[l, 1, grp, n].reshape(256, C)
            st = lax.dot_general(kv[l, :, 0:C], qc, NT, preferred_element_type=F32)
            dp = lax.dot_general(kv[l, :, C : 2 * C], gc, NT, preferred_element_type=F32)
            peak = jnp.max(st, axis=0, keepdims=True)
            p = jnp.exp(st - peak)
            pbuf[grp, l, n] = p
            dpbuf[grp, l, n] = dp
            total = jnp.sum(p, axis=0, keepdims=True)
            inner = jnp.sum(p * dp, axis=0, keepdims=True)
            for k in range(2):
                cols = slice(128 * k, 128 * k + 128)
                row = pl.ds(l * 8 + 2 * n + k, 1)
                stat_s[grp, 0, row, :] = peak[:, cols]
                stat_s[grp, 1, row, :] = total[:, cols]
                stat_s[grp, 2, row, :] = inner[:, cols]

    def stats_out(grp, phase):
        src = (stat_s if phase == 0 else stat_c).at[grp]
        return [put(src, stat_r.at[grp, phase, d - 1], plane_device(0, phase, d)) for d in range(1, 4)]

    def stats_in(grp, phase, cps):
        arrive(cps)
        src = stat_s if phase == 0 else stat_c
        terms = [(src[grp, 0], src[grp, 1], src[grp, 2])]
        for d in range(3):
            terms.append((stat_r[grp, phase, d, 0], stat_r[grp, phase, d, 1], stat_r[grp, phase, d, 2]))
        peak = jnp.maximum(jnp.maximum(terms[0][0], terms[1][0]), jnp.maximum(terms[2][0], terms[3][0]))
        scale = [jnp.exp(t[0] - peak) for t in terms]
        total = sum(t[1] * f for t, f in zip(terms, scale))
        inner = sum(t[2] * f for t, f in zip(terms, scale))
        if phase == 0:
            stat_c[grp, 0] = peak
            stat_c[grp, 1] = total
            stat_c[grp, 2] = inner
        else:
            fac[grp] = jnp.exp(stat_s[grp, 0] - peak) / total
            inn[grp] = inner / total

    low = lax.broadcasted_iota(jnp.int32, (C, 128), 1) < 64

    def dscores(grp):
        @pl.loop(0, 4)
        def _(n):
            dqc = []
            for l in range(L):
                def row(ref):
                    return jnp.concatenate([ref[grp, pl.ds(l * 8 + 2 * n + k, 1), :] for k in range(2)], axis=1)

                a = pbuf[grp, l, n] * row(fac)
                ds = (a * (dpbuf[grp, l, n] - row(inn))).astype(BF16)
                cols = pl.ds(pl.multiple_of(n * 256, 256), 256)
                dsb[l, :, cols] = ds
                alb[l, :, cols] = a.astype(BF16)
                dqc.append(jnp.dot(kt[l], ds, preferred_element_type=F32))
            for k in range(2):
                one, two = (v[:, 128 * k : 128 * k + 128] for v in dqc)
                even = jnp.where(low, one, pltpu.roll(two, 64, 1)).astype(BF16)
                odd = jnp.where(low, pltpu.roll(one, 64, 1), two).astype(BF16)
                for half in range(2):
                    rows = slice(128 * half, 128 * half + 128)
                    dqs[grp, half, n, 2 * k] = even[rows]
                    dqs[grp, half, n, 2 * k + 1] = odd[rows]

    def kv_grads(grp):
        for l in range(L):
            for k, left in enumerate((dsb, alb)):
                val = jnp.dot(left[l], qg[l, k, grp].reshape(N // 2, C), preferred_element_type=F32)
                if grp == 0:
                    kvacc[l, k] = val
                else:
                    grads[l, :, k * C : k * C + C] = (kvacc[l, k] + val).astype(BF16)

    def rs_first(grp):
        out = []
        for d in range(1, 4):
            out.append(put(dqs.at[grp, 0, (y + d) % 4], r1.at[grp, 0, d - 1], plane_device(0, 0, d)))
            out.append(put(dqs.at[grp, 1, :, (z + d) % 4], r1.at[grp, 1, d - 1], plane_device(1, 0, d)))
        return out

    def rs_second(grp, first):
        arrive(first)
        for half in range(2):
            own_part = dqs[grp, 0, y] if half == 0 else dqs[grp, 1, :, z]
            acc = own_part.astype(F32)
            for d in range(3):
                acc = acc + r1[grp, half, d].astype(F32)
            s1[grp, half] = acc.astype(BF16)
        out = []
        for d in range(1, 4):
            out.append(put(s1.at[grp, 0, (z + d) % 4], r2.at[grp, 0, d - 1], plane_device(0, 1, d)))
            out.append(put(s1.at[grp, 1, (y + d) % 4], r2.at[grp, 1, d - 1], plane_device(1, 1, d)))
        return out

    def rs_end(grp, second):
        arrive(second)
        for half in range(2):
            acc = (s1[grp, 0, z] if half == 0 else s1[grp, 1, y]).astype(F32)
            for d in range(3):
                acc = acc + r2[grp, half, d].astype(F32)
            dqt[grp, :, :, :, 128 * half : 128 * half + 128] = acc.T.reshape(2, 2, 32, 128).astype(BF16)
        if grp == 0:
            mine = load(dqt.at[0, :, core], ob.at[:, tgt, y, z])
            out = [put(dqt.at[0, :, 1 - core], ob.at[:, tgt, y, z], (inp, partner, mdl))]
            return out, mine
        out = []
        for r in range(2):
            c = (core + r) % 2
            out.append(put(dqt.at[1, :, c], ob.at[:, tgt, y, z], (inp, opp + c, mdl)))
        return out, None

    def oview(grp):
        first = xh * 2 if grp == 0 else opp
        return lambda half, yy, zz: ob.at[half, pl.ds(first, 2), yy, zz]

    def store(grp):
        first = xh * 2 if grp == 0 else opp
        return load(ob.at[:, pl.ds(first, 2)], dq_out.at[:, pl.ds(first, 2)])

    def block(xx, cc):
        f = (xx // 2) * 4 + cc * 2 + xx % 2
        rows = pl.ds(pl.multiple_of(f * 512, 512), 512)
        acc = lax.dot_general(grads[0], w[0, rows, :], NT, preferred_element_type=F32)
        acc = acc + lax.dot_general(grads[1], w[1, rows, :], NT, preferred_element_type=F32)
        return acc.astype(BF16)

    def both(k, xx):
        eb[k, 0] = block(xx, 1 - core)
        cp = put(eb.at[k, 0], cr.at[k], at_x(x, 1 - core))
        eb[k, 1] = block(xx, core)
        return cp

    pl.semaphore_wait(barrier, len(friends))

    x_phase, x_whole, core_phase = [], [], []
    for r in range(2):
        there = opp + (core + r) % 2
        device = (inp, there, mdl)
        x_phase.append(put(g_hbm.at[there, 0, y, z], qg.at[0, 1, 1, y, z, core], device))
        x_phase.append(put(q_hbm.at[there, :, y, z], qg.at[:, 0, 1, y, z, core], device))
    for k, src in enumerate((q_hbm, g_hbm)):
        core_phase.append(put(src.at[partner], qg.at[:, k, 0, :, :, core], (inp, partner, mdl)))
    for r in range(2):
        there = opp + (core + r) % 2
        x_whole.append(put(g_hbm.at[there, 1], qg.at[1, 1, 1, :, :, core], (inp, there, mdl)))

    enc_load.wait()
    project(0)
    project(1)
    for cp in own:
        cp.wait()
    arrive(core_phase)
    scores(0, 0)
    scores(0, 1)
    sa = stats_out(0, 0)
    arrive(x_phase)
    q_a0 = gather_phase(qview(0), 0)
    q_a1 = gather_phase(qview(1), 0)
    stats_in(0, 0, sa)
    sa = stats_out(0, 1)
    arrive(q_a0)
    q_b0 = gather_phase(qview(0), 1)
    arrive(q_a1)
    q_b1 = gather_phase(qview(1), 1)
    stats_in(0, 1, sa)
    dscores(0)
    fa = rs_first(0)
    kv_grads(0)
    arrive(q_b0)
    scores(1, 0)
    arrive(q_b1)
    arrive(x_whole)
    scores(1, 1)
    sb = stats_out(1, 0)
    ea = rs_second(0, fa)
    stats_in(1, 0, sb)
    sb = stats_out(1, 1)
    xa, ma = rs_end(0, ea)
    stats_in(1, 1, sb)
    dscores(1)
    fb = rs_first(1)
    arrive(xa)
    ma.wait()
    aa = gather_phase(oview(0), 0)
    kv_grads(1)
    c_o = both(0, xo)
    c_p = both(1, xp)
    arrive([c_o])
    eb[0, 1] = eb[0, 1] + cr[0]
    ro = [
        put(eb.at[0, 1, pl.ds(0, 256)], rl.at[0], at_x(xp, core)),
        put(eb.at[0, 1, pl.ds(256, 256)], rl.at[1], at_x(xm, core)),
    ]
    c_m = both(2, xm)
    arrive(aa)
    ba = gather_phase(oview(0), 1)
    arrive([c_p, c_m])
    eb[1, 1] = eb[1, 1] + cr[1]
    eb[2, 1] = eb[2, 1] + cr[2]
    n1 = [
        put(eb.at[1, 1, pl.ds(256, 256)], nb.at[0, pl.ds(256, 256)], at_x(xp, core)),
        put(eb.at[2, 1, pl.ds(0, 256)], nb.at[1, pl.ds(0, 256)], at_x(xm, core)),
    ]
    e2 = rs_second(1, fb)
    c_s = both(3, x)
    arrive(ro)
    eb[1, 1, 0:256] = eb[1, 1, 0:256] + rl[0]
    eb[2, 1, 256:512] = eb[2, 1, 256:512] + rl[1]
    n2 = [
        put(eb.at[1, 1, pl.ds(0, 256)], nb.at[0, pl.ds(0, 256)], at_x(xp, core)),
        put(eb.at[2, 1, pl.ds(256, 256)], nb.at[1, pl.ds(256, 256)], at_x(xm, core)),
    ]
    xb, _ = rs_end(1, e2)
    arrive(xb)
    ab = gather_phase(oview(1), 0)
    arrive([c_s])
    arrive(ba)
    out_a = store(0)
    arrive(ab)
    bb = gather_phase(oview(1), 1)
    arrive(n1)
    arrive(n2)
    enc_out[...] = (
        eb[3, 1].astype(F32) + cr[3].astype(F32) + nb[0].astype(F32) + nb[1].astype(F32)
    ).astype(BF16)
    arrive(bb)
    out_b = store(1)
    for cp in sent:
        cp.wait_send()
    out_a.wait()
    out_b.wait()


def body(encoder, key_weight, value_weight, queries, grad_out):
    kw = key_weight.reshape(L, D, C)
    vw = value_weight.reshape(L, D, C)
    q = jnp.transpose(queries, (2, 0, 1, 3)).reshape(4, L, 4, 4, 32, C)
    g = jnp.transpose(grad_out, (2, 0, 1, 3)).reshape(4, L, 4, 4, 32, C)
    anywhere = pl.BlockSpec(memory_space=pl.ANY)
    dq, de = pl.pallas_call(
        kernel,
        out_shape=(
            jax.ShapeDtypeStruct((L, 4, 4, 4, 32, C), BF16),
            jax.ShapeDtypeStruct((E, 512), BF16),
        ),
        in_specs=[anywhere] * 5,
        out_specs=(anywhere, pl.BlockSpec(memory_space=pltpu.VMEM)),
        scratch_shapes=[
            pltpu.VMEM((E, D), BF16),
            pltpu.VMEM((L, D, 2 * C), BF16),
            pltpu.VMEM((L, 2, 2, 4, 4, 2, 32, C), BF16),
            pltpu.VMEM((L, E, 2 * C), BF16),
            pltpu.VMEM((L, C, E), BF16),
            pltpu.VMEM((2, L, 4, E, 256), F32),
            pltpu.VMEM((2, L, 4, E, 256), F32),
            pltpu.VMEM((L, E, N // 2), BF16),
            pltpu.VMEM((L, E, N // 2), BF16),
            pltpu.VMEM((2, 3, 16, 128), F32),
            pltpu.VMEM((2, 2, 3, 3, 16, 128), F32),
            pltpu.VMEM((2, 3, 16, 128), F32),
            pltpu.VMEM((2, 16, 128), F32),
            pltpu.VMEM((2, 16, 128), F32),
            pltpu.VMEM((2, 2, 4, 4, 128, 128), BF16),
            pltpu.VMEM((2, 2, 3, 4, 128, 128), BF16),
            pltpu.VMEM((2, 2, 4, 128, 128), BF16),
            pltpu.VMEM((2, 2, 3, 128, 128), BF16),
            pltpu.VMEM((2, L, 2, 32, C), BF16),
            pltpu.VMEM((L, 4, 4, 4, 32, C), BF16),
            pltpu.VMEM((L, 2, E, C), F32),
            pltpu.VMEM((L, E, 2 * C), BF16),
            pltpu.VMEM((4, 2, E, 512), BF16),
            pltpu.VMEM((4, E, 512), BF16),
            pltpu.VMEM((2, 256, 512), BF16),
            pltpu.VMEM((2, E, 512), BF16),
            pltpu.SemaphoreType.DMA((NSEM,)),
            pltpu.SemaphoreType.DMA((NSEM,)),
            pltpu.SemaphoreType.DMA((16,)),
        ],
        compiler_params=pltpu.CompilerParams(
            collective_id=0, has_side_effects=True, vmem_limit_bytes=60 * 2**20
        ),
        cost_estimate=pl.CostEstimate(flops=14_000_000_000, bytes_accessed=20_000_000, transcendentals=2_000_000),
    )(encoder, kw, vw, q, g)
    dq = jnp.transpose(dq.reshape(L, 4, 512, C), (0, 2, 1, 3))
    return dq, de


def solution(mesh):
    placed = (
        P("inp", None),
        P(None, None, "mdl", "tgt", None),
        P(None, None, "mdl", "tgt", None),
        P(None, "tgt", "mdl", None),
        P(None, "tgt", "mdl", None),
    )
    return jax.shard_map(
        body,
        mesh=mesh,
        in_specs=placed,
        out_specs=(P(None, "tgt", "mdl", None), P("inp", ("tgt", "mdl"))),
        check_vma=False,
    )
```

time: 102 us -> 98.4 us (0.965)
  Pallas kernels: 91.1 us -> 87.3 us
    pallas_call x1, Pallas kernels: 91.1 us -> 87.3 us  [body(): pl.pallas_call(kernel, out_shape=(jax.ShapeDtypeStruct((L, 4, 4, 4, 32, C...]
where the time goes in v2:
time: 98.4 us; the launch traced here: 98.3 us
  Pallas kernels  87.3 us (89%)
  local copies, waits for them, and re-layouts  10.3 us (10%)
    pallas_call x1, Pallas kernels, body(): pl.pallas_call(kernel, out_shape=(jax.ShapeDtypeStruct((L, 4, 4, 4, 32, C...  87.3 us
    reshape x1, local copies, waits for them, and re-layouts, body(): dq = jnp.transpose(dq.reshape(L, 4, 512, C), (0, 2, 1, 3))  4.59 us
    transpose x1, local copies, waits for them, and re-layouts, body(): q = jnp.transpose(queries, (2, 0, 1, 3)).reshape(4, L, 4, 4, 32, C)  3.33 us

profile of v2, /device:TPU:1, one launch (start us, length us, event | category | flops | bytes accessed | tf_op | source)
XLA Modules:
  0.0 98.3 jit_solution(9343798897766784155)
XLA Ops:
  0.6 0.0 copy-start
  0.6 3.3 %copy.7 = bf16[4,2,512,256]{3,2,1,0:T(8,128)(2,1)} copy(bf16[4,2,512,256]{3,0,2,1:T(4,128)(2,1)} %bitcast.10) | data formatting | bytes 4194304 | tf_op jit(solution)/shard_map/transpose | solution.py:358
  4.0 0.0 copy-done
  4.0 1.6 %copy.8 = bf16[4,2,512,256]{3,2,1,0:T(8,128)(2,1)} copy(bf16[4,2,512,256]{3,0,2,1:T(4,128)(2,1)S(1)} %bitcast.11) | data formatting | bytes 4194304 | tf_op jit(solution)/shard_map/transpose | solution.py:359
  5.6 87.3 %shard_map.68 = (bf16[2,4,4,4,32,256]{5,4,3,2,1,0:T(8,128)(2,1)}, bf16[512,512]{1,0:T(8,128)(2,1)}) custom-call(bf16[512,4096]{1,0:T(8,128)(2,1)} %enc_hbm.1, bf16[2,4096,256]{2,1,0:T(8,128)(2,1)} %bitcast.16, bf16[2,4096,256]{2,1,0:T(8,128)(2,1)} %bitcast.17, bf16[4,2,4,4,32,256]{5,4,3,2,1,0:T(8,128)(2,1)} %bitcast.14, bf16[4,2,4,4,32,256]{5,4,3,2,1,0:T(8,128)(2,1)} %bitcast.15), custom_call_target="tpu_custom_call" | custom-call | flops 14000000000 | bytes 20000000 | tf_op jit(solution)/shard_map/pallas_call | solution.py:361
  92.9 0.0 copy-start.1
  92.9 4.6 %copy.11 = bf16[2,4,512,256]{3,1,2,0:T(4,128)(2,1)} copy(bf16[2,4,512,256]{3,2,1,0:T(8,128)(2,1)} %bitcast.13) | data formatting | bytes 4194304 | tf_op jit(solution)/shard_map/reshape | solution.py:405
  97.5 0.0 copy-done.1
  97.5 0.8 copy.13
Async XLA Ops:
  0.6 3.3 %copy-start = (bf16[2,512,4,256]{3,2,1,0:T(4,128)(2,1)S(1)}, bf16[2,512,4,256]{3,2,1,0:T(4,128)(2,1)}, u32[]{:S(2)}) copy-start(bf16[2,512,4,256]{3,2,1,0:T(4,128)(2,1)} %param.9) | copy-start | bytes 6291460
  92.9 4.6 %copy-start.1 = (bf16[512,512]{1,0:T(8,128)(2,1)S(1)}, bf16[512,512]{1,0:T(8,128)(2,1)}, u32[]{:S(2)}) copy-start(bf16[512,512]{1,0:T(8,128)(2,1)} %get-tuple-element.9) | copy-start | bytes 1572868

commit v3 on v2

--- a/solution.py
+++ b/solution.py
@@ -17,7 +17,7 @@
 C = 256
 L = 2
 N = 2048
-NSEM = 128
+NSEM = 108
 
 
 def kernel(
@@ -92,17 +92,18 @@
             return at_yz((y + d) % 4, z)
         return at_yz(y, (z + d) % 4)
 
-    def gather_phase(view, phase):
+    def gather_phase(view, phase, to=None):
+        to = to or view
         out = []
         for d in range(1, 4):
             for half in range(2):
                 if phase == 0:
-                    ref = view(half, y, z)
+                    place = (half, y, z)
                 elif half == 0:
-                    ref = view(half, slice(None), z)
+                    place = (half, slice(None), z)
                 else:
-                    ref = view(half, y, slice(None))
-                out.append(put(ref, ref, plane_device(half, phase, d)))
+                    place = (half, y, slice(None))
+                out.append(put(view(*place), to(*place), plane_device(half, phase, d)))
         return out
 
     def qview(l):
@@ -230,13 +231,14 @@
             out.append(put(dqt.at[1, :, c], ob.at[:, tgt, y, z], (inp, opp + c, mdl)))
         return out, None
 
-    def oview(grp):
+    def oview(grp, ref=ob):
         first = xh * 2 if grp == 0 else opp
-        return lambda half, yy, zz: ob.at[half, pl.ds(first, 2), yy, zz]
-
-    def store(grp):
-        first = xh * 2 if grp == 0 else opp
-        return load(ob.at[:, pl.ds(first, 2)], dq_out.at[:, pl.ds(first, 2)])
+        return lambda half, yy, zz: ref.at[half, pl.ds(first, 2), yy, zz]
+
+    def spread(grp):
+        out = gather_phase(oview(grp), 1, oview(grp, dq_out))
+        lines = ((0, slice(None), z), (1, y, slice(None)))
+        return out, [load(oview(grp)(*line), oview(grp, dq_out)(*line)) for line in lines]
 
     def block(xx, cc):
         f = (xx // 2) * 4 + cc * 2 + xx % 2
@@ -261,12 +263,12 @@
         x_phase.append(put(q_hbm.at[there, :, y, z], qg.at[:, 0, 1, y, z, core], device))
     for k, src in enumerate((q_hbm, g_hbm)):
         core_phase.append(put(src.at[partner], qg.at[:, k, 0, :, :, core], (inp, partner, mdl)))
+
+    enc_load.wait()
+    project(0)
     for r in range(2):
         there = opp + (core + r) % 2
         x_whole.append(put(g_hbm.at[there, 1], qg.at[1, 1, 1, :, :, core], (inp, there, mdl)))
-
-    enc_load.wait()
-    project(0)
     project(1)
     for cp in own:
         cp.wait()
@@ -313,8 +315,9 @@
         put(eb.at[0, 1, pl.ds(256, 256)], rl.at[1], at_x(xm, core)),
     ]
     c_m = both(2, xm)
+    e2 = rs_second(1, fb)
     arrive(aa)
-    ba = gather_phase(oview(0), 1)
+    ba, out_a = spread(0)
     arrive([c_p, c_m])
     eb[1, 1] = eb[1, 1] + cr[1]
     eb[2, 1] = eb[2, 1] + cr[2]
@@ -322,7 +325,7 @@
         put(eb.at[1, 1, pl.ds(256, 256)], nb.at[0, pl.ds(256, 256)], at_x(xp, core)),
         put(eb.at[2, 1, pl.ds(0, 256)], nb.at[1, pl.ds(0, 256)], at_x(xm, core)),
     ]
-    e2 = rs_second(1, fb)
+    xb, _ = rs_end(1, e2)
     c_s = both(3, x)
     arrive(ro)
     eb[1, 1, 0:256] = eb[1, 1, 0:256] + rl[0]
@@ -331,25 +334,22 @@
         put(eb.at[1, 1, pl.ds(0, 256)], nb.at[0, pl.ds(0, 256)], at_x(xp, core)),
         put(eb.at[2, 1, pl.ds(256, 256)], nb.at[1, pl.ds(256, 256)], at_x(xm, core)),
     ]
-    xb, _ = rs_end(1, e2)
     arrive(xb)
     ab = gather_phase(oview(1), 0)
     arrive([c_s])
-    arrive(ba)
-    out_a = store(0)
     arrive(ab)
-    bb = gather_phase(oview(1), 1)
+    bb, out_b = spread(1)
     arrive(n1)
     arrive(n2)
     enc_out[...] = (
         eb[3, 1].astype(F32) + cr[3].astype(F32) + nb[0].astype(F32) + nb[1].astype(F32)
     ).astype(BF16)
+    arrive(ba)
     arrive(bb)
-    out_b = store(1)
     for cp in sent:
         cp.wait_send()
-    out_a.wait()
-    out_b.wait()
+    for cp in out_a + out_b:
+        cp.wait()
 
 
 def body(encoder, key_weight, value_weight, queries, grad_out):

time: 98.4 us -> 93.2 us (0.947)
  Pallas kernels: 87.3 us -> 82 us
    pallas_call x1, Pallas kernels: 87.3 us -> 82 us  [body(): pl.pallas_call(kernel, out_shape=(jax.ShapeDtypeStruct((L, 4, 4, 4, 32, C...]
where the time goes in v3:
time: 93.2 us; the launch traced here: 93 us
  Pallas kernels  82 us (88%)
  local copies, waits for them, and re-layouts  10.3 us (11%)
    pallas_call x1, Pallas kernels, body(): pl.pallas_call(kernel, out_shape=(jax.ShapeDtypeStruct((L, 4, 4, 4, 32, C...  82 us
    reshape x1, local copies, waits for them, and re-layouts, body(): dq = jnp.transpose(dq.reshape(L, 4, 512, C), (0, 2, 1, 3))  4.59 us
    transpose x1, local copies, waits for them, and re-layouts, body(): q = jnp.transpose(queries, (2, 0, 1, 3)).reshape(4, L, 4, 4, 32, C)  3.33 us

profile of v3, /device:TPU:1, one launch (start us, length us, event | category | flops | bytes accessed | tf_op | source)
XLA Modules:
  0.0 93.0 jit_solution(12237741315056570699)
XLA Ops:
  0.6 0.0 copy-start
  0.6 3.3 %copy.7 = bf16[4,2,512,256]{3,2,1,0:T(8,128)(2,1)} copy(bf16[4,2,512,256]{3,0,2,1:T(4,128)(2,1)} %bitcast.10) | data formatting | bytes 4194304 | tf_op jit(solution)/shard_map/transpose | solution.py:358
  4.0 0.0 copy-done
  4.0 1.6 %copy.8 = bf16[4,2,512,256]{3,2,1,0:T(8,128)(2,1)} copy(bf16[4,2,512,256]{3,0,2,1:T(4,128)(2,1)S(1)} %bitcast.11) | data formatting | bytes 4194304 | tf_op jit(solution)/shard_map/transpose | solution.py:359
  5.6 82.0 %shard_map.68 = (bf16[2,4,4,4,32,256]{5,4,3,2,1,0:T(8,128)(2,1)}, bf16[512,512]{1,0:T(8,128)(2,1)}) custom-call(bf16[512,4096]{1,0:T(8,128)(2,1)} %enc_hbm.1, bf16[2,4096,256]{2,1,0:T(8,128)(2,1)} %bitcast.16, bf16[2,4096,256]{2,1,0:T(8,128)(2,1)} %bitcast.17, bf16[4,2,4,4,32,256]{5,4,3,2,1,0:T(8,128)(2,1)} %bitcast.14, bf16[4,2,4,4,32,256]{5,4,3,2,1,0:T(8,128)(2,1)} %bitcast.15), custom_call_target="tpu_custom_call" | custom-call | flops 14000000000 | bytes 20000000 | tf_op jit(solution)/shard_map/pallas_call | solution.py:361
  87.6 0.0 copy-start.1
  87.6 4.6 %copy.11 = bf16[2,4,512,256]{3,1,2,0:T(4,128)(2,1)} copy(bf16[2,4,512,256]{3,2,1,0:T(8,128)(2,1)} %bitcast.13) | data formatting | bytes 4194304 | tf_op jit(solution)/shard_map/reshape | solution.py:405
  92.2 0.0 copy-done.1
  92.2 0.8 copy.13
Async XLA Ops:
  0.6 3.3 %copy-start = (bf16[2,512,4,256]{3,2,1,0:T(4,128)(2,1)S(1)}, bf16[2,512,4,256]{3,2,1,0:T(4,128)(2,1)}, u32[]{:S(2)}) copy-start(bf16[2,512,4,256]{3,2,1,0:T(4,128)(2,1)} %param.9) | copy-start | bytes 6291460
  87.6 4.6 %copy-start.1 = (bf16[512,512]{1,0:T(8,128)(2,1)S(1)}, bf16[512,512]{1,0:T(8,128)(2,1)}, u32[]{:S(2)}) copy-start(bf16[512,512]{1,0:T(8,128)(2,1)} %get-tuple-element.9) | copy-start | bytes 1572868

commit v4 on v3

--- a/solution.py
+++ b/solution.py
@@ -107,9 +107,7 @@
         return out
 
     def qview(l):
-        if l == 0:
-            return lambda half, yy, zz: qg.at[0, half, 1, yy, zz]
-        return lambda half, yy, zz: qg.at[1, 0, 1, yy, zz, half]
+        return lambda half, yy, zz: qg.at[l, half, 1, yy, zz]
 
     def project(l):
         for cp in w_loads[l]:
@@ -260,7 +258,7 @@
         there = opp + (core + r) % 2
         device = (inp, there, mdl)
         x_phase.append(put(g_hbm.at[there, 0, y, z], qg.at[0, 1, 1, y, z, core], device))
-        x_phase.append(put(q_hbm.at[there, :, y, z], qg.at[:, 0, 1, y, z, core], device))
+        x_phase.append(put(q_hbm.at[there, 0, y, z], qg.at[0, 0, 1, y, z, core], device))
     for k, src in enumerate((q_hbm, g_hbm)):
         core_phase.append(put(src.at[partner], qg.at[:, k, 0, :, :, core], (inp, partner, mdl)))
 
@@ -268,7 +266,8 @@
     project(0)
     for r in range(2):
         there = opp + (core + r) % 2
-        x_whole.append(put(g_hbm.at[there, 1], qg.at[1, 1, 1, :, :, core], (inp, there, mdl)))
+        for k, src in enumerate((q_hbm, g_hbm)):
+            x_whole.append(put(src.at[there, 1], qg.at[1, k, 1, :, :, core], (inp, there, mdl)))
     project(1)
     for cp in own:
         cp.wait()
@@ -278,20 +277,16 @@
     sa = stats_out(0, 0)
     arrive(x_phase)
     q_a0 = gather_phase(qview(0), 0)
-    q_a1 = gather_phase(qview(1), 0)
     stats_in(0, 0, sa)
     sa = stats_out(0, 1)
     arrive(q_a0)
     q_b0 = gather_phase(qview(0), 1)
-    arrive(q_a1)
-    q_b1 = gather_phase(qview(1), 1)
     stats_in(0, 1, sa)
     dscores(0)
     fa = rs_first(0)
     kv_grads(0)
     arrive(q_b0)
     scores(1, 0)
-    arrive(q_b1)
     arrive(x_whole)
     scores(1, 1)
     sb = stats_out(1, 0)

time: 93.2 us -> 92.6 us (level)
  no operation moved by 1% of the time
where the time goes in v4:
time: 92.6 us; the launch traced here: 92.4 us
  Pallas kernels  81.4 us (88%)
  local copies, waits for them, and re-layouts  10.3 us (11%)
    pallas_call x1, Pallas kernels, body(): pl.pallas_call(kernel, out_shape=(jax.ShapeDtypeStruct((L, 4, 4, 4, 32, C...  81.4 us
    reshape x1, local copies, waits for them, and re-layouts, body(): dq = jnp.transpose(dq.reshape(L, 4, 512, C), (0, 2, 1, 3))  4.59 us
    transpose x1, local copies, waits for them, and re-layouts, body(): q = jnp.transpose(queries, (2, 0, 1, 3)).reshape(4, L, 4, 4, 32, C)  3.33 us

profile of v4, /device:TPU:1, one launch (start us, length us, event | category | flops | bytes accessed | tf_op | source)
XLA Modules:
  0.0 92.4 jit_solution(12535060052321129326)
XLA Ops:
  0.6 0.0 copy-start
  0.6 3.3 %copy.7 = bf16[4,2,512,256]{3,2,1,0:T(8,128)(2,1)} copy(bf16[4,2,512,256]{3,0,2,1:T(4,128)(2,1)} %bitcast.10) | data formatting | bytes 4194304 | tf_op jit(solution)/shard_map/transpose | solution.py:353
  4.0 0.0 copy-done
  4.0 1.6 %copy.8 = bf16[4,2,512,256]{3,2,1,0:T(8,128)(2,1)} copy(bf16[4,2,512,256]{3,0,2,1:T(4,128)(2,1)S(1)} %bitcast.11) | data formatting | bytes 4194304 | tf_op jit(solution)/shard_map/transpose | solution.py:354
  5.6 81.4 %shard_map.68 = (bf16[2,4,4,4,32,256]{5,4,3,2,1,0:T(8,128)(2,1)}, bf16[512,512]{1,0:T(8,128)(2,1)}) custom-call(bf16[512,4096]{1,0:T(8,128)(2,1)} %enc_hbm.1, bf16[2,4096,256]{2,1,0:T(8,128)(2,1)} %bitcast.16, bf16[2,4096,256]{2,1,0:T(8,128)(2,1)} %bitcast.17, bf16[4,2,4,4,32,256]{5,4,3,2,1,0:T(8,128)(2,1)} %bitcast.14, bf16[4,2,4,4,32,256]{5,4,3,2,1,0:T(8,128)(2,1)} %bitcast.15), custom_call_target="tpu_custom_call" | custom-call | flops 14000000000 | bytes 20000000 | tf_op jit(solution)/shard_map/pallas_call | solution.py:356
  87.0 0.0 copy-start.1
  87.0 4.6 %copy.11 = bf16[2,4,512,256]{3,1,2,0:T(4,128)(2,1)} copy(bf16[2,4,512,256]{3,2,1,0:T(8,128)(2,1)} %bitcast.13) | data formatting | bytes 4194304 | tf_op jit(solution)/shard_map/reshape | solution.py:400
  91.6 0.0 copy-done.1
  91.6 0.8 copy.13
Async XLA Ops:
  0.6 3.3 %copy-start = (bf16[2,512,4,256]{3,2,1,0:T(4,128)(2,1)S(1)}, bf16[2,512,4,256]{3,2,1,0:T(4,128)(2,1)}, u32[]{:S(2)}) copy-start(bf16[2,512,4,256]{3,2,1,0:T(4,128)(2,1)} %param.9) | copy-start | bytes 6291460
  87.0 4.6 %copy-start.1 = (bf16[512,512]{1,0:T(8,128)(2,1)S(1)}, bf16[512,512]{1,0:T(8,128)(2,1)}, u32[]{:S(2)}) copy-start(bf16[512,512]{1,0:T(8,128)(2,1)} %get-tuple-element.9) | copy-start | bytes 1572868

commit v5 on v4

--- a/solution.py
+++ b/solution.py
@@ -261,13 +261,13 @@
         x_phase.append(put(q_hbm.at[there, 0, y, z], qg.at[0, 0, 1, y, z, core], device))
     for k, src in enumerate((q_hbm, g_hbm)):
         core_phase.append(put(src.at[partner], qg.at[:, k, 0, :, :, core], (inp, partner, mdl)))
-
-    enc_load.wait()
-    project(0)
     for r in range(2):
         there = opp + (core + r) % 2
         for k, src in enumerate((q_hbm, g_hbm)):
             x_whole.append(put(src.at[there, 1], qg.at[1, k, 1, :, :, core], (inp, there, mdl)))
+
+    enc_load.wait()
+    project(0)
     project(1)
     for cp in own:
         cp.wait()

time: 92.6 us -> 92 us (level)
  no operation moved by 1% of the time
where the time goes in v5:
time: 92 us; the launch traced here: 91.8 us
  Pallas kernels  80.8 us (88%)
  local copies, waits for them, and re-layouts  10.3 us (11%)
    pallas_call x1, Pallas kernels, body(): pl.pallas_call(kernel, out_shape=(jax.ShapeDtypeStruct((L, 4, 4, 4, 32, C...  80.8 us
    reshape x1, local copies, waits for them, and re-layouts, body(): dq = jnp.transpose(dq.reshape(L, 4, 512, C), (0, 2, 1, 3))  4.59 us
    transpose x1, local copies, waits for them, and re-layouts, body(): q = jnp.transpose(queries, (2, 0, 1, 3)).reshape(4, L, 4, 4, 32, C)  3.33 us

profile of v5, /device:TPU:1, one launch (start us, length us, event | category | flops | bytes accessed | tf_op | source)
XLA Modules:
  0.0 91.8 jit_solution(5535464744341427434)
XLA Ops:
  0.6 0.0 copy-start
  0.6 3.3 %copy.7 = bf16[4,2,512,256]{3,2,1,0:T(8,128)(2,1)} copy(bf16[4,2,512,256]{3,0,2,1:T(4,128)(2,1)} %bitcast.10) | data formatting | bytes 4194304 | tf_op jit(solution)/shard_map/transpose | solution.py:353
  4.0 0.0 copy-done
  4.0 1.6 %copy.8 = bf16[4,2,512,256]{3,2,1,0:T(8,128)(2,1)} copy(bf16[4,2,512,256]{3,0,2,1:T(4,128)(2,1)S(1)} %bitcast.11) | data formatting | bytes 4194304 | tf_op jit(solution)/shard_map/transpose | solution.py:354
  5.6 80.8 %shard_map.68 = (bf16[2,4,4,4,32,256]{5,4,3,2,1,0:T(8,128)(2,1)}, bf16[512,512]{1,0:T(8,128)(2,1)}) custom-call(bf16[512,4096]{1,0:T(8,128)(2,1)} %enc_hbm.1, bf16[2,4096,256]{2,1,0:T(8,128)(2,1)} %bitcast.16, bf16[2,4096,256]{2,1,0:T(8,128)(2,1)} %bitcast.17, bf16[4,2,4,4,32,256]{5,4,3,2,1,0:T(8,128)(2,1)} %bitcast.14, bf16[4,2,4,4,32,256]{5,4,3,2,1,0:T(8,128)(2,1)} %bitcast.15), custom_call_target="tpu_custom_call" | custom-call | flops 14000000000 | bytes 20000000 | tf_op jit(solution)/shard_map/pallas_call | solution.py:356
  86.4 0.0 copy-start.1
  86.4 4.6 %copy.11 = bf16[2,4,512,256]{3,1,2,0:T(4,128)(2,1)} copy(bf16[2,4,512,256]{3,2,1,0:T(8,128)(2,1)} %bitcast.13) | data formatting | bytes 4194304 | tf_op jit(solution)/shard_map/reshape | solution.py:400
  91.0 0.0 copy-done.1
  91.0 0.8 copy.13
Async XLA Ops:
  0.6 3.3 %copy-start = (bf16[2,512,4,256]{3,2,1,0:T(4,128)(2,1)S(1)}, bf16[2,512,4,256]{3,2,1,0:T(4,128)(2,1)}, u32[]{:S(2)}) copy-start(bf16[2,512,4,256]{3,2,1,0:T(4,128)(2,1)} %param.9) | copy-start | bytes 6291460
  86.4 4.6 %copy-start.1 = (bf16[512,512]{1,0:T(8,128)(2,1)S(1)}, bf16[512,512]{1,0:T(8,128)(2,1)}, u32[]{:S(2)}) copy-start(bf16[512,512]{1,0:T(8,128)(2,1)} %get-tuple-element.9) | copy-start | bytes 1572868
